TPU v7x, 32 devices: a whole 2x2x4 slice. The times are simulated.
32 devices in a mesh: gx: 4 (over x, core), gy: 8 (over z, y).
Axes of the slice: x: 2, y: 2, z: 4, core: 2. Of those that a mesh axis runs over, the one named last changes fastest.
Arguments:
- nest_state: float32 [4, 8, 96, 3072], P(None, None, 'gx', 'gy'), may hold values from -6 to 6
- parent_state: float32 [4, 8, 96, 3072], P(None, None, 'gx', 'gy'), may hold values from -6 to 6
- offset_x: int32 [1], replicated, may hold values from 1 to 15
- offset_y: int32 [1], replicated, may hold values from 385 to 511
Outputs:
- nest_out: float32 [4, 8, 96, 3072], P(None, None, 'gx', 'gy')
- parent_out: float32 [4, 8, 96, 3072], P(None, None, 'gx', 'gy')
All inputs are finite; a program needn't handle non-finite values.
Results may differ from a plain program's by a relative error of at most 0.00019.
Values sent between devices are 32-bit elements; how exact they have to be, the bound alone decides.
A program may use at most 128 MiB of HBM per device.

v0:
```python
import jax
import jax.numpy as jnp
from jax import lax
from jax.sharding import PartitionSpec as P

SUBSTEPS = 3


CARRY_RATE = 0.35
SOUND_RATE = 0.4
MIXING_RATE = 0.2


def extended(value, sides, width):
    for axis, dim in sides:
        size, length = (lax.axis_size(axis), value.shape[dim])
        up = [(i, (i + 1) % size) for i in range(size - 1)]
        down = [(j, i) for i, j in up]
        last = lax.slice_in_dim(value, length - width, length, axis=dim)
        initial = lax.slice_in_dim(value, 0, width, axis=dim)
        before = lax.ppermute(last, axis, up)
        after = lax.ppermute(initial, axis, down)
        value = jnp.concatenate([before, value, after], axis=dim)
    return value


def advance(padded):
    center = padded[:, :, 1:-1, 1:-1]
    slope_x = (padded[:, :, 2:, 1:-1] - padded[:, :, :-2, 1:-1]) * 0.5
    slope_y = (padded[:, :, 1:-1, 2:] - padded[:, :, 1:-1, :-2]) * 0.5
    carried = center[0][None] * slope_x[:3] + center[1][None] * slope_y[:3]
    potential = center[2]
    level_above = jnp.concatenate([potential[1:], potential[-1:]], axis=0)
    level_below = jnp.concatenate([potential[:1], potential[:-1]], axis=0)
    wind_east = center[0] - CARRY_RATE * carried[0] - SOUND_RATE * slope_x[3]
    wind_north = center[1] - CARRY_RATE * carried[1] - SOUND_RATE * slope_y[3]
    heat_next = (
        potential
        - CARRY_RATE * carried[2]
        + MIXING_RATE * (level_above - 2.0 * potential + level_below)
    )
    pressure = center[3] - SOUND_RATE * (slope_x[0] + slope_y[1])
    return jnp.stack([wind_east, wind_north, heat_next, pressure])


def place_along(piece, first, width, axis):
    length = piece.shape[axis]
    target = lax.broadcasted_iota(jnp.int32, (length, width), 0) - first
    places = lax.broadcasted_iota(jnp.int32, (length, width), 1)
    table = (target == places).astype(jnp.float32)
    moved = jnp.moveaxis(piece, axis, -1)
    placed = jnp.dot(
        moved, table, precision=lax.Precision.HIGHEST, preferred_element_type=jnp.float32
    )
    return jnp.moveaxis(placed, -1, axis)


def on_device(nest_state, parent_state, offset_x, offset_y):
    shift_x = offset_x[0]
    shift_y = offset_y[0]
    count_x = lax.axis_size("gx")
    count_y = lax.axis_size("gy")
    index_x = lax.axis_index("gx")
    index_y = lax.axis_index("gy")
    levels = nest_state.shape[1]
    nest_cols = nest_state.shape[2]
    nest_rows = nest_state.shape[3]
    parent_cols = parent_state.shape[2]
    parent_rows = parent_state.shape[3]
    coarse_cols = nest_cols // 3
    coarse_rows = nest_rows // 3
    span_x = count_x * coarse_cols
    span_y = count_y * coarse_rows

    def take_slab(wanted, owner_index, extent, axis):
        local = wanted - owner_index * extent
        inside = (local >= 0) & (local < extent)
        slab = lax.dynamic_slice_in_dim(parent_state, jnp.clip(local, 0, extent - 1), 1, axis)
        return jnp.where(inside, jnp.squeeze(slab, axis), 0.0)

    columns = jnp.stack(
        [
            take_slab(shift_x - 1, index_x, parent_cols, 2),
            take_slab(shift_x + span_x, index_x, parent_cols, 2),
        ]
    )
    columns = lax.psum(columns, "gx")
    row_pair = jnp.stack(
        [
            take_slab(shift_y - 1, index_y, parent_rows, 3),
            take_slab(shift_y + span_y, index_y, parent_rows, 3),
        ]
    )
    row_pair = lax.psum(row_pair, "gy")
    column_first = shift_y + index_y * coarse_rows - 1
    row_first = shift_x + index_x * coarse_cols - 1
    column_strip = place_along(
        lax.all_gather(columns, "gy", axis=3, tiled=True), column_first, coarse_rows + 2, 3
    )
    row_strip = place_along(
        lax.all_gather(row_pair, "gx", axis=3, tiled=True), row_first, coarse_cols + 2, 3
    )
    column_strip = jnp.repeat(column_strip, 3, axis=3)
    row_strip = jnp.repeat(row_strip, 3, axis=3)
    parent_padded = extended(parent_state, (("gx", 2), ("gy", 3)), 1)
    parent_next = advance(parent_padded)
    fields = nest_state
    for substep in range(SUBSTEPS):
        padded = extended(fields, (("gx", 2), ("gy", 3)), 1)
        col_pos = lax.broadcasted_iota(jnp.int32, (padded.shape[2], 1), 0)
        row_pos = lax.broadcasted_iota(jnp.int32, (1, padded.shape[3]), 1)
        lower = 3 - 1
        west = column_strip[0][:, :, None, lower : lower + nest_rows + 2 * 1]
        east = column_strip[1][:, :, None, lower : lower + nest_rows + 2 * 1]
        south = row_strip[0][:, :, lower : lower + nest_cols + 2 * 1, None]
        north = row_strip[1][:, :, lower : lower + nest_cols + 2 * 1, None]
        result = jnp.where((index_x == 0) & (col_pos < 1), west, padded)
        result = jnp.where((index_x == count_x - 1) & (col_pos >= nest_cols + 1), east, result)
        result = jnp.where((index_y == 0) & (row_pos < 1), south, result)
        result = jnp.where((index_y == count_y - 1) & (row_pos >= nest_rows + 1), north, result)
        fields = advance(result)
    coarse = fields[:3].reshape(3, levels, coarse_cols, 3, coarse_rows, 3).mean(axis=(3, 5))
    col_first = index_x * parent_cols - shift_x
    rows_first = index_y * parent_rows - shift_y
    partial_block = place_along(
        lax.all_gather(coarse, "gy", axis=3, tiled=True), rows_first, parent_rows, 3
    )
    returned = place_along(
        lax.all_gather(partial_block, "gx", axis=2, tiled=True), col_first, parent_cols, 2
    )
    col_global = index_x * parent_cols + lax.broadcasted_iota(jnp.int32, (parent_cols, 1), 0)
    row_global = index_y * parent_rows + lax.broadcasted_iota(jnp.int32, (1, parent_rows), 1)
    inside = (
        (col_global >= shift_x)
        & (col_global < shift_x + span_x)
        & (row_global >= shift_y)
        & (row_global < shift_y + span_y)
    )
    blended = jnp.where(inside, returned, parent_next[:3])
    parent_out = jnp.concatenate([blended, parent_next[3:]], axis=0)
    return (fields, parent_out)


def solution(mesh):
    placed = (P(None, None, "gx", "gy"), P(None, None, "gx", "gy"), P(), P())
    return jax.shard_map(
        on_device,
        mesh=mesh,
        in_specs=placed,
        out_specs=(P(None, None, "gx", "gy"), P(None, None, "gx", "gy")),
        check_vma=False,
    )
```

profile of v0, /device:TPU:9, one launch (start us, length us, event | category | flops | bytes accessed | tf_op | source)
XLA Modules:
  0.0 319.7 jit_solution(11506212641012016978)
XLA Ops:
  8.0 2.1 fusion.95
  12.0 3.8 %collective-permute-start = (f32[4,8,1,384]{3,2,1,0:T(1,128)S(1)}, f32[4,8,1,384]{3,2,1,0:T(1,128)S(1)}, u32[]{:S(2)}, u32[]{:S(2)}) collective-permute-start(f32[4,8,1,384]{3,2,1,0:T(1,128)S(1)} %get-tuple-element.68), channel_id=1, source_target_pairs={{0,8},{8,16},{16,24},{1,9},{9,17},{17,25},{2,10},{10,18},{18,26},{... | collective-permute-start | bytes 147464 | tf_op jit(solution)/shard_map/ppermute | solution.py:21
  15.9 1.9 collective-permute-start.1
  19.5 28.2 %psum.14 = f32[2,4,8,24]{2,1,0,3:T(4,128)S(1)} all-reduce(f32[2,4,8,24]{2,1,0,3:T(4,128)S(1)} %copy.41), channel_id=1, replica_groups=mesh['gx'=4,'gy'=8] {'gy'}, use_global_device_ids=true, to_apply=%region_0.1 | all-reduce | flops 1536 | bytes 12288 | tf_op jit(solution)/shard_map/psum | solution.py:94
  47.7 14.2 %all_gather.12 = f32[2,4,8,96]{2,1,0,3:T(4,128)S(1)} all-gather(f32[2,4,8,24]{2,1,0,3:T(4,128)S(1)} %psum.14), channel_id=1, replica_groups=mesh['gx'=4,'gy'=8] {'gx'}, dimensions={3}, use_global_device_ids=true | all-gather | bytes 30720 | tf_op jit(solution)/shard_map/all_gather | solution.py:101
  66.1 4.3 %collective-permute-start.3 = (f32[4,8,26,1]{3,2,1,0:T(8,128)}, f32[4,8,26,1]{3,2,1,0:T(8,128)}, u32[]{:S(2)}, u32[]{:S(2)}) collective-permute-start(f32[4,8,26,1]{3,2,1,0:T(8,128)} %get-tuple-element.51), channel_id=1, source_target_pairs={{1,0},{2,1},{3,2},{4,3},{5,4},{6,5},{7,6},{9,8},{10,9},{11,10},{12... | collective-permute-start | bytes 9992 | tf_op jit(solution)/shard_map/ppermute | solution.py:22
  70.4 41.6 %all_gather.13 = f32[2,4,8,3072]{3,2,1,0:T(8,128)S(1)} all-gather(f32[2,4,8,384]{3,2,1,0:T(8,128)} %all-reduce.2.cloned.1.call-done), channel_id=1, replica_groups=mesh['gx'=4,'gy'=8] {'gy'}, dimensions={3}, use_global_device_ids=true | all-gather | bytes 884736 | tf_op jit(solution)/shard_map/all_gather | solution.py:98
  114.5 3.1 fusion.2
  120.0 8.7 %collective-permute-start.4 = (f32[4,8,1,384]{3,2,1,0:T(1,128)S(1)}, f32[4,8,1,384]{3,2,1,0:T(1,128)S(1)}, u32[]{:S(2)}, u32[]{:S(2)}) collective-permute-start(f32[4,8,1,384]{3,2,1,0:T(1,128)S(1)} %get-tuple-element.64), channel_id=1, source_target_pairs={{0,8},{8,16},{16,24},{1,9},{9,17},{17,25},{2,10},{10,18},{18,26},{... | collective-permute-start | bytes 147464 | tf_op jit(solution)/shard_map/ppermute | solution.py:21
  128.8 1.9 collective-permute-start.5
  132.6 3.6 %collective-permute-start.13 = (f32[4,8,1,384]{3,2,1,0:T(1,128)}, f32[4,8,1,384]{3,2,1,0:T(1,128)S(1)}, u32[]{:S(2)}, u32[]{:S(2)}) collective-permute-start(f32[4,8,1,384]{3,2,1,0:T(1,128)} %get-tuple-element.58), channel_id=1, source_target_pairs={{0,8},{8,16},{16,24},{1,9},{9,17},{17,25},{2,10},{10,18},{18,26},{... | collective-permute-start | bytes 147464 | tf_op jit(solution)/shard_map/ppermute | solution.py:21
  136.6 1.9 collective-permute-start.6
  138.5 4.4 %collective-permute-start.7 = (f32[4,8,26,1]{3,2,1,0:T(8,128)S(1)}, f32[4,8,26,1]{3,2,1,0:T(8,128)S(1)}, u32[]{:S(2)}, u32[]{:S(2)}) collective-permute-start(f32[4,8,26,1]{3,2,1,0:T(8,128)S(1)} %get-tuple-element.49), channel_id=1, source_target_pairs={{1,0},{2,1},{3,2},{4,3},{5,4},{6,5},{7,6},{9,8},{10,9},{11,10},{12... | collective-permute-start | bytes 9992 | tf_op jit(solution)/shard_map/ppermute | solution.py:22
  143.8 16.6 %collective-permute-done.6 = f32[4,8,26,1]{3,2,1,0:T(8,128)S(1)} collective-permute-done((f32[4,8,26,1]{3,2,1,0:T(8,128)S(1)}, f32[4,8,26,1]{3,2,1,0:T(8,128)S(1)}, u32[]{:S(2)}, u32[]{:S(2)}) %collective-permute-start.6) | collective-permute-done | bytes 3360 | tf_op jit(solution)/shard_map/ppermute | solution.py:21
  160.4 3.3 %collective-permute-done.7 = f32[4,8,26,1]{3,2,1,0:T(8,128)S(1)} collective-permute-done((f32[4,8,26,1]{3,2,1,0:T(8,128)S(1)}, f32[4,8,26,1]{3,2,1,0:T(8,128)S(1)}, u32[]{:S(2)}, u32[]{:S(2)}) %collective-permute-start.7) | collective-permute-done | bytes 3360 | tf_op jit(solution)/shard_map/ppermute | solution.py:22
  163.7 2.6 fusion.5
  168.7 2.5 collective-permute-start.8
  171.2 1.9 collective-permute-start.9
  173.8 2.8 collective-permute-done.9
  176.9 1.9 collective-permute-start.10
  178.9 4.3 %collective-permute-start.11 = (f32[4,8,26,1]{3,2,1,0:T(8,128)S(1)}, f32[4,8,26,1]{3,2,1,0:T(8,128)S(1)}, u32[]{:S(2)}, u32[]{:S(2)}) collective-permute-start(f32[4,8,26,1]{3,2,1,0:T(8,128)S(1)} %get-tuple-element.47), channel_id=1, source_target_pairs={{1,0},{2,1},{3,2},{4,3},{5,4},{6,5},{7,6},{9,8},{10,9},{11,10},{12... | collective-permute-start | bytes 9992 | tf_op jit(solution)/shard_map/ppermute | solution.py:22
  183.1 16.6 %collective-permute-done.10 = f32[4,8,26,1]{3,2,1,0:T(8,128)S(1)} collective-permute-done((f32[4,8,26,1]{3,2,1,0:T(8,128)S(1)}, f32[4,8,26,1]{3,2,1,0:T(8,128)S(1)}, u32[]{:S(2)}, u32[]{:S(2)}) %collective-permute-start.10) | collective-permute-done | bytes 3360 | tf_op jit(solution)/shard_map/ppermute | solution.py:21
  199.7 3.3 %collective-permute-done.11 = f32[4,8,26,1]{3,2,1,0:T(8,128)S(1)} collective-permute-done((f32[4,8,26,1]{3,2,1,0:T(8,128)S(1)}, f32[4,8,26,1]{3,2,1,0:T(8,128)S(1)}, u32[]{:S(2)}, u32[]{:S(2)}) %collective-permute-start.11) | collective-permute-done | bytes 3360 | tf_op jit(solution)/shard_map/ppermute | solution.py:22
  203.0 2.6 fusion.8
  208.6 8.3 %copy.53 = f32[3,8,24,384]{1,3,2,0:T(8,128)} copy(f32[3,8,24,384]{3,2,1,0:T(8,128)S(1)} %pad_maximum_fusion.10) | data formatting | bytes 1769472 | tf_op jit(solution)/shard_map/stack | solution.py:43
  216.9 21.9 %reshape.170 = f32[3,8,8,3,128,3]{1,5,4,3,2,0:T(4,128)} reshape(f32[3,8,24,384]{1,3,2,0:T(8,128)} %copy.53) | data formatting | bytes 1769472 | tf_op jit(solution)/shard_map/reshape | solution.py:122
  238.7 14.8 %reduce_sum.9 = f32[3,8,8,128]{1,3,2,0:T(8,128)S(1)} reduce(f32[3,8,8,3,128,3]{1,5,4,3,2,0:T(4,128)} %reshape.170, f32[]{:T(128)} %constant.17.clone.1), dimensions={3,5}, to_apply=%region_2.3 | reduce | flops 196608 | bytes 983044 | tf_op jit(solution)/shard_map/reduce_sum | solution.py:122
  254.0 24.0 %all_gather.14 = f32[3,8,8,1024]{3,2,1,0:T(8,128)S(1)} all-gather(f32[3,8,8,128]{3,2,1,0:T(8,128)S(1)} %broadcast_multiply_fusion), channel_id=1, replica_groups=mesh['gx'=4,'gy'=8] {'gy'}, dimensions={3}, use_global_device_ids=true | all-gather | bytes 884736 | tf_op jit(solution)/shard_map/all_gather | solution.py:126
  280.2 3.8 %collective-permute-start.14 = (f32[4,8,26,1]{3,2,1,0:T(8,128)S(1)}, f32[4,8,26,1]{3,2,1,0:T(8,128)S(1)}, u32[]{:S(2)}, u32[]{:S(2)}) collective-permute-start(f32[4,8,26,1]{3,2,1,0:T(8,128)S(1)} %get-tuple-element.44), channel_id=1, source_target_pairs={{1,0},{2,1},{3,2},{4,3},{5,4},{6,5},{7,6},{9,8},{10,9},{11,10},{12... | collective-permute-start | bytes 9992 | tf_op jit(solution)/shard_map/ppermute | solution.py:22
  284.0 1.9 collective-permute-start.15
  286.0 16.4 %collective-permute-done.14 = f32[4,8,26,1]{3,2,1,0:T(8,128)S(1)} collective-permute-done((f32[4,8,26,1]{3,2,1,0:T(8,128)S(1)}, f32[4,8,26,1]{3,2,1,0:T(8,128)S(1)}, u32[]{:S(2)}, u32[]{:S(2)}) %collective-permute-start.14) | collective-permute-done | bytes 3360 | tf_op jit(solution)/shard_map/ppermute | solution.py:22
  302.4 3.1 collective-permute-done.15
  (112 shorter events, 31.1 us)
Async XLA Ops:
  7.2 11.3 %copy-start = (f32[4,8,24,384]{3,2,1,0:T(8,128)S(1)}, f32[4,8,24,384]{3,2,1,0:T(8,128)}, u32[]{:S(2)}) copy-start(f32[4,8,24,384]{3,2,1,0:T(8,128)} %param.5) | copy-start | bytes 3538948
  7.2 63.2 %all-reduce.2.cloned.1.call-start = ((), (), s32[]{:S(2)}) async-start(), calls=%async_computation | async-start | bytes 196608 | tf_op jit(solution)/shard_map/psum | solution.py:87
  10.8 299.1 %all-gather.2.cloned.1.call-start = ((), (), s32[]{:S(2)}) async-start(), calls=%async_computation.1 | async-start | bytes 1474560 | tf_op jit(solution)/shard_map/all_gather | solution.py:129
  12.0 50.8 %collective-permute-start = (f32[4,8,1,384]{3,2,1,0:T(1,128)S(1)}, f32[4,8,1,384]{3,2,1,0:T(1,128)S(1)}, u32[]{:S(2)}, u32[]{:S(2)}) collective-permute-start(f32[4,8,1,384]{3,2,1,0:T(1,128)S(1)} %get-tuple-element.68), channel_id=1, source_target_pairs={{0,8},{8,16},{16,24},{1,9},{9,17},{17,25},{2,10},{10,18},{18,26},{... | collective-permute-start | bytes 147464 | tf_op jit(solution)/shard_map/ppermute | solution.py:21
  15.9 47.0 %collective-permute-start.1 = (f32[4,8,1,384]{3,2,1,0:T(1,128)S(1)}, f32[4,8,1,384]{3,2,1,0:T(1,128)S(1)}, u32[]{:S(2)}, u32[]{:S(2)}) collective-permute-start(f32[4,8,1,384]{3,2,1,0:T(1,128)S(1)} %get-tuple-element.69), channel_id=1, source_target_pairs={{8,0},{16,8},{24,16},{9,1},{17,9},{25,17},{10,2},{18,10},{26,18},{... | collective-permute-start | bytes 147464 | tf_op jit(solution)/shard_map/ppermute | solution.py:22
  19.0 43.9 %copy-start.1 = (f32[4,8,24,384]{3,2,1,0:T(8,128)S(1)}, f32[4,8,24,384]{3,2,1,0:T(8,128)}, u32[]{:S(2)}) copy-start(f32[4,8,24,384]{3,2,1,0:T(8,128)} %param.4) | copy-start | bytes 3538948
  64.2 50.4 %collective-permute-start.2 = (f32[4,8,26,1]{3,2,1,0:T(8,128)}, f32[4,8,26,1]{3,2,1,0:T(8,128)}, u32[]{:S(2)}, u32[]{:S(2)}) collective-permute-start(f32[4,8,26,1]{3,2,1,0:T(8,128)} %get-tuple-element.50), channel_id=1, source_target_pairs={{0,1},{1,2},{2,3},{3,4},{4,5},{5,6},{6,7},{8,9},{9,10},{10,11},{11... | collective-permute-start | bytes 9992 | tf_op jit(solution)/shard_map/ppermute | solution.py:21
  66.1 48.5 %collective-permute-start.3 = (f32[4,8,26,1]{3,2,1,0:T(8,128)}, f32[4,8,26,1]{3,2,1,0:T(8,128)}, u32[]{:S(2)}, u32[]{:S(2)}) collective-permute-start(f32[4,8,26,1]{3,2,1,0:T(8,128)} %get-tuple-element.51), channel_id=1, source_target_pairs={{1,0},{2,1},{3,2},{4,3},{5,4},{6,5},{7,6},{9,8},{10,9},{11,10},{12... | collective-permute-start | bytes 9992 | tf_op jit(solution)/shard_map/ppermute | solution.py:22
  120.0 16.3 %collective-permute-start.4 = (f32[4,8,1,384]{3,2,1,0:T(1,128)S(1)}, f32[4,8,1,384]{3,2,1,0:T(1,128)S(1)}, u32[]{:S(2)}, u32[]{:S(2)}) collective-permute-start(f32[4,8,1,384]{3,2,1,0:T(1,128)S(1)} %get-tuple-element.64), channel_id=1, source_target_pairs={{0,8},{8,16},{16,24},{1,9},{9,17},{17,25},{2,10},{10,18},{18,26},{... | collective-permute-start | bytes 147464 | tf_op jit(solution)/shard_map/ppermute | solution.py:21
  128.8 7.5 %collective-permute-start.5 = (f32[4,8,1,384]{3,2,1,0:T(1,128)S(1)}, f32[4,8,1,384]{3,2,1,0:T(1,128)S(1)}, u32[]{:S(2)}, u32[]{:S(2)}) collective-permute-start(f32[4,8,1,384]{3,2,1,0:T(1,128)S(1)} %get-tuple-element.65), channel_id=1, source_target_pairs={{8,0},{16,8},{24,16},{9,1},{17,9},{25,17},{10,2},{18,10},{26,18},{... | collective-permute-start | bytes 147464 | tf_op jit(solution)/shard_map/ppermute | solution.py:22
  130.7 149.2 %collective-permute-start.12 = (f32[4,8,1,384]{3,2,1,0:T(1,128)}, f32[4,8,1,384]{3,2,1,0:T(1,128)S(1)}, u32[]{:S(2)}, u32[]{:S(2)}) collective-permute-start(f32[4,8,1,384]{3,2,1,0:T(1,128)} %get-tuple-element.59), channel_id=1, source_target_pairs={{8,0},{16,8},{24,16},{9,1},{17,9},{25,17},{10,2},{18,10},{26,18},{... | collective-permute-start | bytes 147464 | tf_op jit(solution)/shard_map/ppermute | solution.py:22
  132.6 147.3 %collective-permute-start.13 = (f32[4,8,1,384]{3,2,1,0:T(1,128)}, f32[4,8,1,384]{3,2,1,0:T(1,128)S(1)}, u32[]{:S(2)}, u32[]{:S(2)}) collective-permute-start(f32[4,8,1,384]{3,2,1,0:T(1,128)} %get-tuple-element.58), channel_id=1, source_target_pairs={{0,8},{8,16},{16,24},{1,9},{9,17},{17,25},{2,10},{10,18},{18,26},{... | collective-permute-start | bytes 147464 | tf_op jit(solution)/shard_map/ppermute | solution.py:21
  136.6 23.8 %collective-permute-start.6 = (f32[4,8,26,1]{3,2,1,0:T(8,128)S(1)}, f32[4,8,26,1]{3,2,1,0:T(8,128)S(1)}, u32[]{:S(2)}, u32[]{:S(2)}) collective-permute-start(f32[4,8,26,1]{3,2,1,0:T(8,128)S(1)} %get-tuple-element.48), channel_id=1, source_target_pairs={{0,1},{1,2},{2,3},{3,4},{4,5},{5,6},{6,7},{8,9},{9,10},{10,11},{11... | collective-permute-start | bytes 9992 | tf_op jit(solution)/shard_map/ppermute | solution.py:21
  138.5 25.2 %collective-permute-start.7 = (f32[4,8,26,1]{3,2,1,0:T(8,128)S(1)}, f32[4,8,26,1]{3,2,1,0:T(8,128)S(1)}, u32[]{:S(2)}, u32[]{:S(2)}) collective-permute-start(f32[4,8,26,1]{3,2,1,0:T(8,128)S(1)} %get-tuple-element.49), channel_id=1, source_target_pairs={{1,0},{2,1},{3,2},{4,3},{5,4},{6,5},{7,6},{9,8},{10,9},{11,10},{12... | collective-permute-start | bytes 9992 | tf_op jit(solution)/shard_map/ppermute | solution.py:22
  168.7 5.1 %collective-permute-start.8 = (f32[4,8,1,384]{3,2,1,0:T(1,128)S(1)}, f32[4,8,1,384]{3,2,1,0:T(1,128)S(1)}, u32[]{:S(2)}, u32[]{:S(2)}) collective-permute-start(f32[4,8,1,384]{3,2,1,0:T(1,128)S(1)} %get-tuple-element.62), channel_id=1, source_target_pairs={{0,8},{8,16},{16,24},{1,9},{9,17},{17,25},{2,10},{10,18},{18,26},{... | collective-permute-start | bytes 147464 | tf_op jit(solution)/shard_map/ppermute | solution.py:21
  171.2 5.4 %collective-permute-start.9 = (f32[4,8,1,384]{3,2,1,0:T(1,128)S(1)}, f32[4,8,1,384]{3,2,1,0:T(1,128)S(1)}, u32[]{:S(2)}, u32[]{:S(2)}) collective-permute-start(f32[4,8,1,384]{3,2,1,0:T(1,128)S(1)} %get-tuple-element.63), channel_id=1, source_target_pairs={{8,0},{16,8},{24,16},{9,1},{17,9},{25,17},{10,2},{18,10},{26,18},{... | collective-permute-start | bytes 147464 | tf_op jit(solution)/shard_map/ppermute | solution.py:22
  176.9 22.8 %collective-permute-start.10 = (f32[4,8,26,1]{3,2,1,0:T(8,128)S(1)}, f32[4,8,26,1]{3,2,1,0:T(8,128)S(1)}, u32[]{:S(2)}, u32[]{:S(2)}) collective-permute-start(f32[4,8,26,1]{3,2,1,0:T(8,128)S(1)} %get-tuple-element.46), channel_id=1, source_target_pairs={{0,1},{1,2},{2,3},{3,4},{4,5},{5,6},{6,7},{8,9},{9,10},{10,11},{11... | collective-permute-start | bytes 9992 | tf_op jit(solution)/shard_map/ppermute | solution.py:21
  178.9 24.1 %collective-permute-start.11 = (f32[4,8,26,1]{3,2,1,0:T(8,128)S(1)}, f32[4,8,26,1]{3,2,1,0:T(8,128)S(1)}, u32[]{:S(2)}, u32[]{:S(2)}) collective-permute-start(f32[4,8,26,1]{3,2,1,0:T(8,128)S(1)} %get-tuple-element.47), channel_id=1, source_target_pairs={{1,0},{2,1},{3,2},{4,3},{5,4},{6,5},{7,6},{9,8},{10,9},{11,10},{12... | collective-permute-start | bytes 9992 | tf_op jit(solution)/shard_map/ppermute | solution.py:22
  208.5 8.3 %copy-start.2 = (f32[1,8,24,384]{3,2,1,0:T(8,128)}, f32[1,8,24,384]{3,2,1,0:T(8,128)S(1)}, u32[]{:S(2)}) copy-start(f32[1,8,24,384]{3,2,1,0:T(8,128)S(1)} %get-tuple-element.11) | copy-start | bytes 884740
  280.2 22.2 %collective-permute-start.14 = (f32[4,8,26,1]{3,2,1,0:T(8,128)S(1)}, f32[4,8,26,1]{3,2,1,0:T(8,128)S(1)}, u32[]{:S(2)}, u32[]{:S(2)}) collective-permute-start(f32[4,8,26,1]{3,2,1,0:T(8,128)S(1)} %get-tuple-element.44), channel_id=1, source_target_pairs={{1,0},{2,1},{3,2},{4,3},{5,4},{6,5},{7,6},{9,8},{10,9},{11,10},{12... | collective-permute-start | bytes 9992 | tf_op jit(solution)/shard_map/ppermute | solution.py:22
  284.0 21.4 %collective-permute-start.15 = (f32[4,8,26,1]{3,2,1,0:T(8,128)S(1)}, f32[4,8,26,1]{3,2,1,0:T(8,128)S(1)}, u32[]{:S(2)}, u32[]{:S(2)}) collective-permute-start(f32[4,8,26,1]{3,2,1,0:T(8,128)S(1)} %get-tuple-element.45), channel_id=1, source_target_pairs={{0,1},{1,2},{2,3},{3,4},{4,5},{5,6},{6,7},{8,9},{9,10},{10,11},{11... | collective-permute-start | bytes 9992 | tf_op jit(solution)/shard_map/ppermute | solution.py:21
  306.7 0.9 copy-start.6
  306.7 1.1 copy-start.7
  306.7 1.1 copy-start.8
  306.7 1.1 copy-start.9
  307.8 1.0 copy-start.3
  307.8 1.0 copy-start.4
  308.8 1.1 copy-start.5
Sparse Core Ops, SparseCore 0:
  10.9 31.5 all-reduce.1
  279.8 23.9 all-gather.1
where the time goes:
time: 325 us; the launch traced here: 320 us
  blocking collectives  108 us (33%)
  waiting for transfers between devices  62.2 us (19%)
  starting transfers between devices  50.9 us (16%)
  local copies, waits for them, and re-layouts  40.7 us (13%)
  other arithmetic  36.6 us (11%)
  between operations  16.1 us (5%)
  matrix products  5.11 us (2%)
    all_gather x1, blocking collectives, on_device(): lax.all_gather(columns, 'gy', axis=3, tiled=True)  41.6 us
    ppermute x8, waiting for transfers between devices, extended(): before = lax.ppermute(last, axis, up)  36.3 us
    psum x1, blocking collectives, on_device(): row_pair = lax.psum(row_pair, 'gy')  28.2 us
    ppermute x8, starting transfers between devices, extended(): before = lax.ppermute(last, axis, up)  26.4 us
    ppermute x8, waiting for transfers between devices, extended(): after = lax.ppermute(initial, axis, down)  25.8 us
    ppermute x8, starting transfers between devices, extended(): after = lax.ppermute(initial, axis, down)  24.5 us
    all_gather x1, blocking collectives, on_device(): lax.all_gather(coarse, 'gy', axis=3, tiled=True)  24 us
    reshape x1, local copies, waits for them, and re-layouts, on_device(): fields[:3].reshape(3, levels, coarse_cols, 3, coarse_rows, 3)  21.9 us
  transfers between devices with their start and end apart: 18, of which 7 were waited for; matrix products, arithmetic and copies ran while one was open for 22% of the time, Pallas kernels for 0%

commit v1 on v0

v1 whole, which is shorter than its diff:
```python
import functools

import jax
import jax.numpy as jnp
from jax import lax
from jax.experimental import pallas as pl
from jax.experimental.pallas import tpu as pltpu
from jax.sharding import PartitionSpec as P

SUBSTEPS = 3
CARRY_RATE = 0.35
SOUND_RATE = 0.4
MIXING_RATE = 0.2
MESH = pl.DeviceIdType.MESH
F32 = jnp.float32


def quotient(a, b):
    return a // b if isinstance(a, int) else lax.div(a, jnp.int32(b))


class Line:
    def __init__(self, count, parent, nest, lowest):
        self.count, self.parent, self.nest = count, parent, nest
        self.coarse = nest // 3
        span = count * self.coarse
        self.span = span
        self.low = max(lowest, (count // 2 - 1) * parent - span)
        self.high = max(self.low, min(count * parent - span, (count // 2) * parent - span) - 1)
        self.lift = self.high // self.coarse + 2
        tiles = range(count)
        self.slots = max(self.last(i) - self.first(i) + 1 for i in tiles)
        hit = [(t, i) for i in tiles for t in range(self.first(i), self.last(i) + 1)]
        assert all(0 <= t < count for t, _ in hit)
        self.sources = max(i - self.base(t) + 1 for t, i in hit)
        assert min(i - self.base(t) for t, i in hit) >= 0
        reach = max(parent * t - self.coarse * self.base(t) - self.low for t, _ in hit) + parent
        self.window = max(self.sources, -(-reach // self.coarse)) * self.coarse
        self.tile_low, self.tile_high = self.first(0), self.last(count - 1)
        self.before = ((self.low - 1) // parent, (self.high - 1) // parent)
        self.after = ((self.low + span) // parent, (self.high + span) // parent)
        assert self.before[1] < self.after[0]

    def first(self, i):
        return quotient(self.low + self.coarse * i - 1, self.parent)

    def last(self, i):
        return quotient(self.high + self.coarse * i + self.coarse, self.parent)

    def base(self, t):
        return quotient(self.parent * t - self.high - 1 + self.lift * self.coarse, self.coarse) - self.lift


def kernel(lx, ly, levels, off_x, off_y, nest, parent, nest_out, parent_out,
           fa, fb, pp, xs, xr, ys, yr, cs, cr, rs, rr, gx, gy, coarse, back,
           s_halo, r_halo, s_col, r_col, s_row, r_row, s_back, r_back):
    ix, iy = lax.axis_index("gx"), lax.axis_index("gy")
    ox, oy = off_x[0], off_y[0]
    cols, rows = lx.nest, ly.nest
    wide, high = fa.shape[3], fa.shape[2]
    fields = levels * 4
    n_before = lx.before[1] - lx.before[0] + 1
    n_after = lx.after[1] - lx.after[0] + 1
    n_col = max(n_before, n_after)

    def there(tx, ty):
        return {"gx": tx, "gy": ty}

    def send(ok, src, dst, ssem, rsem, tx, ty, local=True):
        mine = (tx == ix) & (ty == iy)

        @pl.when(ok & jnp.logical_not(mine))
        def _():
            pltpu.make_async_remote_copy(src, dst, ssem, rsem, device_id=there(tx, ty), device_id_type=MESH).start()

        if local:
            @pl.when(ok & mine)
            def _():
                pltpu.make_async_copy(src, dst, rsem).start()

    def sent(ok, src, ssem, tx, ty):
        @pl.when(ok & jnp.logical_not((tx == ix) & (ty == iy)))
        def _():
            pltpu.make_async_copy(src, src, ssem).wait()

    def arrived(ok, dst, rsem, blank=True):
        @pl.when(ok)
        def _():
            pltpu.make_async_copy(dst, dst, rsem).wait()

        if blank:
            @pl.when(jnp.logical_not(ok))
            def _():
                dst[...] = jnp.zeros(dst.shape, F32)

    lane = lax.broadcasted_iota(jnp.int32, (1, 128), 1)

    in_rows = (iy >= ly.tile_low) & (iy <= ly.tile_high)
    in_cols = (ix >= lx.tile_low) & (ix <= lx.tile_high)
    gives_west = (ix >= lx.before[0]) & (ix <= lx.before[1])
    gives_east = (ix >= lx.after[0]) & (ix <= lx.after[1])
    gives_col = in_rows & (gives_west | gives_east)
    col_to = jnp.where(gives_west, 0, lx.count - 1)
    col_slot = ix - jnp.where(gives_west, lx.before[0], lx.after[0])
    gives_south = iy == ly.before[0]
    gives_north = iy == ly.after[0]
    gives_row = in_cols & (gives_south | gives_north)
    row_to = jnp.where(gives_south, 0, ly.count - 1)

    @pl.when(gives_col)
    def _():
        want = ox + jnp.where(gives_west, -1, lx.span) - lx.parent * ix
        sub = lax.broadcasted_iota(jnp.int32, (lx.parent, ly.parent), 0)
        hit = sub == want

        def body(k, _):
            for c in range(4):
                line = jnp.sum(jnp.where(hit, parent[c, k], 0.0), axis=0, keepdims=True)
                cs[pl.ds(c * levels + k, 1), :] = line
            return 0

        lax.fori_loop(0, levels, body, 0)

    def col_targets():
        for j in range(ly.sources):
            ty = ly.base(iy) + j
            tyc = jnp.clip(ty, 0, ly.count - 1)
            ok = gives_col & (ty >= 0) & (ty < ly.count) & (iy >= ly.first(tyc)) & (iy <= ly.last(tyc))
            yield ok, j, tyc, jnp.clip(iy - ly.first(tyc), 0, ly.slots - 1)

    for ok, j, ty, part in col_targets():
        slot = jnp.clip(col_slot, 0, n_col - 1)
        send(ok, cs, cr.at[slot, part], s_col.at[j], r_col.at[slot, part], col_to, ty)

    @pl.when(gives_row)
    def _():
        want = oy + jnp.where(gives_south, -1, ly.span) - ly.parent * iy
        hit = lax.broadcasted_iota(jnp.int32, (lx.parent, ly.parent), 1) == want

        def body(k, acc):
            for c in range(4):
                line = jnp.sum(jnp.where(hit, parent[c, k], 0.0), axis=1, keepdims=True)
                acc = jnp.where(lane == c * levels + k, line, acc)
            return acc

        rs[...] = lax.fori_loop(0, levels, body, jnp.zeros((lx.parent, 128), F32))

    def row_targets():
        for j in range(lx.sources):
            tx = lx.base(ix) + j
            txc = jnp.clip(tx, 0, lx.count - 1)
            ok = gives_row & (tx >= 0) & (tx < lx.count) & (ix >= lx.first(txc)) & (ix <= lx.last(txc))
            yield ok, j, txc, jnp.clip(ix - lx.first(txc), 0, lx.slots - 1)

    for ok, j, tx, part in row_targets():
        send(ok, rs, rr.at[part], s_row.at[j], r_row.at[part], tx, row_to)

    half = levels // 2

    def pack_x(k, _):
        for c in range(4):
            for part in range(2):
                lev = k + part * half
                r = 4 * part
                xs[0, c, k, r:r + 3, :] = nest[c, lev, 0:3, :]
                xs[0, c, k, r + 3:r + 4, :] = parent[c, lev, 0:1, :]
                xs[1, c, k, r:r + 3, :] = nest[c, lev, cols - 3:cols, :]
                xs[1, c, k, r + 3:r + 4, :] = parent[c, lev, cols - 1:cols, :]
        return 0

    lax.fori_loop(0, half, pack_x, 0)

    has = {-1: lambda i, n: i > 0, 0: lambda i, n: i >= 0, 1: lambda i, n: i < n - 1}

    def neighbour(dx, dy):
        ok = has[dx](ix, lx.count) & has[dy](iy, ly.count)
        return ok, jnp.clip(ix + dx, 0, lx.count - 1), jnp.clip(iy + dy, 0, ly.count - 1)

    def halo_sends():
        for n, (dx, dy) in enumerate([(-1, 0), (1, 0), (0, -1), (0, 1), (-1, -1), (-1, 1), (1, -1), (1, 1)]):
            ok, tx, ty = neighbour(dx, dy)
            if dy == 0:
                src, dst = xs.at[(dx + 1) // 2], xr.at[(dx + 1) // 2]
            else:
                d = (dy + 1) // 2
                if dx == 0:
                    src, dst = ys.at[d], yr.at[d, pl.ds(0, cols)]
                elif dx < 0:
                    src, dst = ys.at[d, pl.ds(0, 8)], yr.at[d, pl.ds(cols, 8)]
                else:
                    src, dst = ys.at[d, pl.ds(cols - 8, 8)], yr.at[d, pl.ds(cols + 8, 8)]
            yield n, dx, dy, ok, tx, ty, src, dst

    for n, dx, dy, ok, tx, ty, src, dst in halo_sends():
        if dy == 0:
            send(ok, src, dst, s_halo.at[n], r_halo.at[n], tx, ty, local=False)

    def pack_y(k, acc):
        low, top = acc
        for c in range(4):
            at = 4 * (c * levels + k)
            mine = (lane >= at) & (lane < at + 4)
            a = jnp.where(lane < 3, nest[c, k, :, 0:128], pltpu.roll(parent[c, k, :, 0:128], 3, 1))
            b = jnp.where(lane < 3, pltpu.roll(nest[c, k, :, rows - 128:rows], 3, 1),
                          pltpu.roll(parent[c, k, :, rows - 128:rows], 4, 1))
            low = jnp.where(mine, pltpu.roll(a, at, 1), low)
            top = jnp.where(mine, pltpu.roll(b, at, 1), top)
        return low, top

    blank = jnp.zeros((cols, 128), F32)
    low, top = lax.fori_loop(0, levels, pack_y, (blank, blank))
    ys[0] = low
    ys[1] = top
    for n, dx, dy, ok, tx, ty, src, dst in halo_sends():
        if dy != 0:
            send(ok, src, dst, s_halo.at[n], r_halo.at[n], tx, ty, local=False)

    def middle(k, _):
        for c in range(4):
            fa[c, k, 0:cols, 0:rows] = nest[c, k]
            pp[c, k, 0:cols, 0:rows] = parent[c, k]
        return 0

    lax.fori_loop(0, levels, middle, 0)

    west, east = ix == 0, ix == lx.count - 1
    south, north = iy == 0, iy == ly.count - 1
    takes_col = west | east
    takes_row = south | north
    for s in range(n_col):
        live = (west & (s < n_before)) | (east & (s < n_after))
        for part in range(ly.slots):
            arrived(live & (ly.first(iy) + part <= ly.last(iy)), cr.at[s, part], r_col.at[s, part])
    for part in range(lx.slots):
        arrived(takes_row & (lx.first(ix) + part <= lx.last(ix)), rr.at[part], r_row.at[part])

    def third(v):
        return (((v + 3) * 21846) >> 16) - 1

    @pl.when(takes_col)
    def _():
        y = lax.broadcasted_iota(jnp.int32, (1, wide), 1)
        y = jnp.where(y < rows + 64, y, y - wide)
        place = oy + ly.coarse * iy - ly.parent * ly.first(iy) + third(y)
        total = jnp.zeros((fields, wide), F32)
        for part in range(ly.slots):
            k = lax.broadcasted_iota(jnp.int32, (ly.parent, wide), 0) + part * ly.parent
            table = jnp.where(k == place, 1.0, 0.0).astype(F32)
            strip = cr[0, part]
            for s in range(1, n_col):
                strip = strip + cr[s, part]
            total = total + jnp.dot(strip, table, precision=lax.Precision.HIGHEST, preferred_element_type=F32)
        gx[...] = total

    @pl.when(takes_row)
    def _():
        total = jnp.zeros((high, 128), F32)
        x = lax.broadcasted_iota(jnp.int32, (high, 1), 0)
        x = jnp.where(x < cols + 4, x, x - high)
        place = ox + lx.coarse * ix - lx.parent * lx.first(ix) + third(x)
        for part in range(lx.slots):
            k = lax.broadcasted_iota(jnp.int32, (high, lx.parent), 1) + part * lx.parent
            table = jnp.where(k == place, 1.0, 0.0).astype(F32)
            total = total + jnp.dot(table, rr[part], precision=lax.Precision.HIGHEST, preferred_element_type=F32)

        def body(k, _):
            for c in range(4):
                turned = pltpu.roll(total, lax.rem(128 - (c * levels + k), 128), 1)
                gy[c, k] = jnp.broadcast_to(turned[:, 0:1], (high, 128))
            return 0

        lax.fori_loop(0, levels, body, 0)

    sub8 = lax.broadcasted_iota(jnp.int32, (8, 1), 0)
    at_x = (sub8 == jnp.where(west, 7, -1)) | (sub8 == jnp.where(east, 0, -1))
    at_y = (lane == jnp.where(south, 127, -1)) | (lane == jnp.where(north, 0, -1))

    def put(dst, c, k, value):
        edge = jnp.where(at_x, gx[pl.ds(c * levels + k, 1), :], value[cols:high, :])
        dst[c, k, 0:cols, 0:rows] = value[0:cols, 0:rows]
        dst[c, k, cols:high, 0:rows] = edge[:, 0:rows]
        dst[c, k, 0:cols, rows:wide] = jnp.where(at_y, gy[c, k, 0:cols, :], value[0:cols, rows:wide])
        dst[c, k, cols:high, rows:wide] = jnp.where(at_y, gy[c, k, cols:high, :], edge[:, rows:wide])

    for n, dx, dy, ok, tx, ty, src, dst in halo_sends():
        back_ok, _, _ = neighbour(-dx, -dy)
        arrived(back_ok, dst, r_halo.at[n])

    def unpack(k, _):
        for c in range(4):
            for part in range(2):
                lev = k + part * half
                r = 4 * part
                fa[c, lev, cols:cols + 3, 0:rows] = xr[0, c, k, r:r + 3, :]
                pp[c, lev, cols:cols + 1, 0:rows] = xr[0, c, k, r + 3:r + 4, :]
                fa[c, lev, high - 3:high, 0:rows] = xr[1, c, k, r:r + 3, :]
                pp[c, lev, high - 1:high, 0:rows] = xr[1, c, k, r + 3:r + 4, :]
        return 0

    lax.fori_loop(0, half, unpack, 0)

    def side(d):
        corner = jnp.where(sub8 < 4, yr[d, cols:cols + 8, :], yr[d, cols + 8:cols + 16, :])
        return jnp.concatenate([yr[d, 0:cols, :], corner], axis=0)

    def unpack_y(k, both):
        after, before = both
        for c in range(4):
            at = 4 * (c * levels + k)
            a = pltpu.roll(after, lax.rem(128 - at, 128), 1)
            b = pltpu.roll(before, lax.rem(253 - at, 128), 1)
            block = jnp.where(lane < 64, a, b)
            fa[c, k, :, rows:wide] = jnp.where(at_y, gy[c, k], block)
            pp[c, k, :, rows:wide] = jnp.where(lane < 64, pltpu.roll(a, 125, 1), pltpu.roll(b, 127, 1))
            fa[c, k, cols:high, :] = jnp.where(at_x, gx[pl.ds(c * levels + k, 1), :], fa[c, k, cols:high, :])
        return both

    lax.fori_loop(0, levels, unpack_y, (side(0), side(1)))

    def advanced(src, k):
        u, v, t, p = (src[c, k] for c in range(4))
        above = src[2, jnp.minimum(k + 1, levels - 1)]
        below = src[2, jnp.maximum(k - 1, 0)]

        def dx(f):
            return pltpu.roll(f, high - 1, 0) - pltpu.roll(f, 1, 0)

        def dy(f):
            return pltpu.roll(f, wide - 1, 1) - pltpu.roll(f, 1, 1)

        ux, vy = dx(u), dy(v)
        hu, hv = u * (CARRY_RATE * 0.5), v * (CARRY_RATE * 0.5)
        s = SOUND_RATE * 0.5
        yield u - (hu * ux + hv * dy(u)) - s * dx(p)
        yield v - (hu * dx(v) + hv * vy) - s * dy(p)
        yield t - (hu * dx(t) + hv * dy(t)) + MIXING_RATE * (above - 2.0 * t + below)
        yield p - s * (ux + vy)

    for src, dst in ((fa, fb), (fb, fa)):
        def step(k, _, src=src, dst=dst):
            for c, value in enumerate(advanced(src, k)):
                put(dst, c, k, value)
            return 0

        lax.fori_loop(0, levels, step, 0)

    k = lax.broadcasted_iota(jnp.int32, (rows, ly.coarse), 0)
    j = lax.broadcasted_iota(jnp.int32, (rows, ly.coarse), 1)
    thirds = jnp.where((k >= 3 * j) & (k < 3 * j + 3), 1.0, 0.0).astype(F32)

    j = lax.broadcasted_iota(jnp.int32, (3 * lx.coarse, 3 * cols), 0)
    k = lax.broadcasted_iota(jnp.int32, (3 * lx.coarse, 3 * cols), 1)
    triples = jnp.where((k >= 3 * j) & (k < 3 * j + 3), 1.0, 0.0).astype(F32)

    def last_step(k, _):
        inner = [value[0:cols, 0:rows] for value in advanced(fa, k)]
        for c in range(4):
            nest_out[c, k] = inner[c]
        sums = jnp.dot(jnp.concatenate(inner[:3], axis=0), thirds, precision=lax.Precision.HIGHEST,
                       preferred_element_type=F32)
        mean = jnp.dot(triples, sums, precision=lax.Precision.HIGHEST, preferred_element_type=F32) * (1.0 / 9.0)
        for c in range(3):
            coarse[c * levels + k] = mean[c * lx.coarse:(c + 1) * lx.coarse, :]
        return 0

    lax.fori_loop(0, levels, last_step, 0)

    def back_targets():
        for a in range(lx.slots):
            for b in range(ly.slots):
                tx, ty = lx.first(ix) + a, ly.first(iy) + b
                ok = (tx <= lx.last(ix)) & (ty <= ly.last(iy))
                tx, ty = jnp.minimum(tx, lx.last(ix)), jnp.minimum(ty, ly.last(iy))
                yield ok, a, b, tx, ty, ix - lx.base(tx), iy - ly.base(ty)

    for ok, a, b, tx, ty, sx, sy in back_targets():
        send(ok, coarse, back.at[sx, sy], s_back.at[a, b], r_back.at[sx, sy], tx, ty)

    def parent_step(k, _):
        for c, value in enumerate(advanced(pp, k)):
            parent_out[c, k] = value[0:lx.parent, 0:ly.parent]
        return 0

    lax.fori_loop(0, levels, parent_step, 0)

    takes_back = in_rows & in_cols
    for a in range(lx.sources):
        for b in range(ly.sources):
            sx, sy = lx.base(ix) + a, ly.base(iy) + b
            sxc, syc = jnp.clip(sx, 0, lx.count - 1), jnp.clip(sy, 0, ly.count - 1)
            ok = takes_back & (sx == sxc) & (sy == syc)
            ok = ok & (ix >= lx.first(sxc)) & (ix <= lx.last(sxc)) & (iy >= ly.first(syc)) & (iy <= ly.last(syc))
            arrived(ok, back.at[a, b], r_back.at[a, b], blank=False)

    @pl.when(takes_back)
    def _():
        col = lax.broadcasted_iota(jnp.int32, (lx.parent, ly.parent), 0) + lx.parent * ix - ox
        row = lax.broadcasted_iota(jnp.int32, (lx.parent, ly.parent), 1) + ly.parent * iy - oy
        inside = (col >= 0) & (col < lx.span) & (row >= 0) & (row < ly.span)
        x0 = lx.parent * ix - lx.coarse * lx.base(ix) - ox
        y0 = ly.parent * iy - ly.coarse * ly.base(iy) - oy
        total = lx.window
        nsy = ly.window // ly.coarse

        def body(k, _):
            for c in range(3):
                f = c * levels + k
                whole = jnp.concatenate(
                    [jnp.concatenate([back[a, b, f] for b in range(nsy)], axis=1) for a in range(total // lx.coarse)],
                    axis=0)
                moved = pltpu.roll(pltpu.roll(whole, total - x0, 0), nsy * ly.coarse - y0, 1)
                parent_out[c, k] = jnp.where(inside, moved[0:lx.parent, 0:ly.parent], parent_out[c, k])
            return 0

        lax.fori_loop(0, levels, body, 0)

    for ok, j, ty, part in col_targets():
        sent(ok, cs, s_col.at[j], col_to, ty)
    for ok, j, tx, part in row_targets():
        sent(ok, rs, s_row.at[j], tx, row_to)
    for n, dx, dy, ok, tx, ty, src, dst in halo_sends():
        sent(ok, src, s_halo.at[n], tx, ty)
    for ok, a, b, tx, ty, sx, sy in back_targets():
        sent(ok, coarse, s_back.at[a, b], tx, ty)


def on_device(lx, ly, nest_state, parent_state, offset_x, offset_y):
    levels = nest_state.shape[1]
    cols, rows = nest_state.shape[2:]
    high, wide = cols + 8, rows + 128
    n_col = max(lx.before[1] - lx.before[0], lx.after[1] - lx.after[0]) + 1
    padded = pltpu.VMEM((4, levels, high, wide), F32)
    dma = pltpu.SemaphoreType.DMA
    nbx, nby = lx.window // lx.coarse, ly.window // ly.coarse
    vm = pl.BlockSpec(memory_space=pltpu.VMEM)
    sm = pl.BlockSpec(memory_space=pltpu.SMEM)
    shape = jax.ShapeDtypeStruct(nest_state.shape, F32)
    return pl.pallas_call(
        functools.partial(kernel, lx, ly, levels),
        out_shape=(shape, shape),
        in_specs=[sm, sm, vm, vm],
        out_specs=(vm, vm),
        scratch_shapes=[
            padded, padded, padded,
            pltpu.VMEM((2, 4, levels // 2, 8, rows), F32),
            pltpu.VMEM((2, 4, levels // 2, 8, rows), F32),
            pltpu.VMEM((2, cols, 128), F32),
            pltpu.VMEM((2, cols + 16, 128), F32),
            pltpu.VMEM((4 * levels, ly.parent), F32),
            pltpu.VMEM((n_col, ly.slots, 4 * levels, ly.parent), F32),
            pltpu.VMEM((lx.parent, 128), F32),
            pltpu.VMEM((lx.slots, lx.parent, 128), F32),
            pltpu.VMEM((4 * levels, wide), F32),
            pltpu.VMEM((4, levels, high, 128), F32),
            pltpu.VMEM((3 * levels, lx.coarse, ly.coarse), F32),
            pltpu.VMEM((nbx, nby, 3 * levels, lx.coarse, ly.coarse), F32),
            dma((8,)), dma((8,)),
            dma((ly.sources,)), dma((n_col, ly.slots)),
            dma((lx.sources,)), dma((lx.slots,)),
            dma((lx.slots, ly.slots)), dma((nbx, nby)),
        ],
        compiler_params=pltpu.CompilerParams(has_side_effects=True, vmem_limit_bytes=48 * 1024 * 1024),
    )(offset_x, offset_y, nest_state, parent_state)


def solution(mesh):
    placed = (P(None, None, "gx", "gy"), P(None, None, "gx", "gy"), P(), P())
    count_x, count_y = mesh.shape["gx"], mesh.shape["gy"]

    def program(nest_state, parent_state, offset_x, offset_y):
        lx = Line(count_x, parent_state.shape[2] // count_x, nest_state.shape[2] // count_x, 1)
        rows = parent_state.shape[3] // count_y
        ly = Line(count_y, rows, nest_state.shape[3] // count_y, rows + 1)
        return jax.shard_map(
            functools.partial(on_device, lx, ly),
            mesh=mesh,
            in_specs=placed,
            out_specs=(P(None, None, "gx", "gy"), P(None, None, "gx", "gy")),
            check_vma=False,
        )(nest_state, parent_state, offset_x, offset_y)

    return program
```

time: 325 us -> 45.6 us (0.14); the launches traced: 320 us -> 45.4 us
  blocking collectives: 108 us -> 0 us
  waiting for transfers between devices: 62.2 us -> 0 us
  starting transfers between devices: 50.9 us -> 0 us
  Pallas kernels: 0 us -> 38.9 us
  other arithmetic: 36.6 us -> 0 us
  local copies, waits for them, and re-layouts: 40.7 us -> 4.56 us
  between operations: 16.1 us -> 1.94 us
  matrix products: 5.11 us -> 0 us
    all_gather x3 -> x0, blocking collectives: 79.8 us -> none  [the longest x1 41.6 us: on_device(): lax.all_gather(columns, 'gy', axis=3, tiled=True)]
    ppermute x16 -> x0, waiting for transfers between devices: 62.1 us -> none  [the longest x8 36.3 us: extended(): before = lax.ppermute(last, axis, up)]
    ppermute x16 -> x0, starting transfers between devices: 50.9 us -> none  [the longest x8 26.4 us: extended(): before = lax.ppermute(last, axis, up)]
    pallas_call x0 -> x1, Pallas kernels: none -> 38.9 us  [on_device(): pl.pallas_call(functools.partial(kernel, lx, ly, levels), out_shape=(shap...]
    psum x1 -> x0, blocking collectives: 28.2 us -> none  [on_device(): row_pair = lax.psum(row_pair, 'gy')]
    reshape x1 -> x0, local copies, waits for them, and re-layouts: 21.9 us -> none  [on_device(): fields[:3].reshape(3, levels, coarse_cols, 3, coarse_rows, 3)]
    reduce_sum x1 -> x0, other arithmetic: 14.8 us -> none  [on_device(): fields[:3].reshape(3, levels, coarse_cols, 3, coarse_rows, 3)]
    another operation x2 -> x0, local copies, waits for them, and re-layouts: 8.38 us -> none  [the longest x1 8.27 us: advance(): return jnp.stack([wind_east, wind_north, heat_next, pressure])]
  transfers between devices with their start and end apart: 18 -> 0, of which waited for: 7 -> 0; matrix products, arithmetic and copies ran while one was open for 22% -> 0% of each run, Pallas kernels for 0% -> 0%
where the time goes in v1:
time: 45.6 us; the launch traced here: 45.4 us
  Pallas kernels  38.9 us (85%)
  local copies, waits for them, and re-layouts  4.56 us (10%)
  between operations  1.94 us (4%)
    pallas_call x1, Pallas kernels, on_device(): pl.pallas_call(functools.partial(kernel, lx, ly, levels), out_shape=(shap...  38.9 us
    unnamed x6, local copies, waits for them, and re-layouts  4.56 us

profile of v1, /device:TPU:9, one launch (start us, length us, event | category | flops | bytes accessed | tf_op | source)
XLA Modules:
  0.0 45.4 jit_solution(17869304383172469554)
XLA Ops:
  1.9 0.0 copy-start
  1.9 1.3 %copy-done = f32[4,8,24,384]{3,2,1,0:T(8,128)S(1)} copy-done((f32[4,8,24,384]{3,2,1,0:T(8,128)S(1)}, f32[4,8,24,384]{3,2,1,0:T(8,128)}, u32[]{:S(2)}) %copy-start) | copy-done | bytes 1179672
  3.2 0.0 copy-start.1
  3.2 1.3 %copy-done.1 = f32[4,8,24,384]{3,2,1,0:T(8,128)S(1)} copy-done((f32[4,8,24,384]{3,2,1,0:T(8,128)S(1)}, f32[4,8,24,384]{3,2,1,0:T(8,128)}, u32[]{:S(2)}) %copy-start.1) | copy-done | bytes 1179672
  4.5 38.9 %shard_map.59 = (f32[4,8,24,384]{3,2,1,0:T(8,128)S(1)}, f32[4,8,24,384]{3,2,1,0:T(8,128)S(1)}) custom-call(s32[1]{0:T(128)S(6)} %copy.8.off_x, s32[1]{0:T(128)S(6)} %copy.9.off_y, f32[4,8,24,384]{3,2,1,0:T(8,128)S(1)} %copy-done, f32[4,8,24,384]{3,2,1,0:T(8,128)S(1)} %copy-done.1), custom_call_target="tpu_custom_call" | custom-call | tf_op jit(solution)/shard_map/pallas_call | solution.py:438
  43.4 1.0 %copy.10 = f32[4,8,24,384]{3,2,1,0:T(8,128)} copy(f32[4,8,24,384]{3,2,1,0:T(8,128)S(1)} %get-tuple-element.4) | data formatting | bytes 2359296
  44.4 1.0 %copy.11 = f32[4,8,24,384]{3,2,1,0:T(8,128)} copy(f32[4,8,24,384]{3,2,1,0:T(8,128)S(1)} %get-tuple-element.5) | data formatting | bytes 2359296
Async XLA Ops:
  1.9 1.3 %copy-start = (f32[4,8,24,384]{3,2,1,0:T(8,128)S(1)}, f32[4,8,24,384]{3,2,1,0:T(8,128)}, u32[]{:S(2)}) copy-start(f32[4,8,24,384]{3,2,1,0:T(8,128)} %nest.1) | copy-start | bytes 3538948
  3.2 1.3 %copy-start.1 = (f32[4,8,24,384]{3,2,1,0:T(8,128)S(1)}, f32[4,8,24,384]{3,2,1,0:T(8,128)}, u32[]{:S(2)}) copy-start(f32[4,8,24,384]{3,2,1,0:T(8,128)} %parent.1) | copy-start | bytes 3538948

commit v2 on v1

--- a/solution.py
+++ b/solution.py
@@ -250,7 +250,8 @@
             for s in range(1, n_col):
                 strip = strip + cr[s, part]
             total = total + jnp.dot(strip, table, precision=lax.Precision.HIGHEST, preferred_element_type=F32)
-        gx[...] = total
+        for b in range(wide // 128):
+            gx[b] = total[:, b * 128:b * 128 + 128]
 
     @pl.when(takes_row)
     def _():
@@ -275,12 +276,15 @@
     at_x = (sub8 == jnp.where(west, 7, -1)) | (sub8 == jnp.where(east, 0, -1))
     at_y = (lane == jnp.where(south, 127, -1)) | (lane == jnp.where(north, 0, -1))
 
-    def put(dst, c, k, value):
-        edge = jnp.where(at_x, gx[pl.ds(c * levels + k, 1), :], value[cols:high, :])
-        dst[c, k, 0:cols, 0:rows] = value[0:cols, 0:rows]
-        dst[c, k, cols:high, 0:rows] = edge[:, 0:rows]
-        dst[c, k, 0:cols, rows:wide] = jnp.where(at_y, gy[c, k, 0:cols, :], value[0:cols, rows:wide])
-        dst[c, k, cols:high, rows:wide] = jnp.where(at_y, gy[c, k, cols:high, :], edge[:, rows:wide])
+    def put(dst, c, k, b, value):
+        at = b * 128
+        edge = jnp.where(at_x, gx[b, pl.ds(c * levels + k, 1), :], value[cols:high, :])
+        inner = value[0:cols, :]
+        if b == wide // 128 - 1:
+            edge = jnp.where(at_y, gy[c, k, cols:high, :], edge)
+            inner = jnp.where(at_y, gy[c, k, 0:cols, :], inner)
+        dst[c, k, 0:cols, at:at + 128] = inner
+        dst[c, k, cols:high, at:at + 128] = edge
 
     for n, dx, dy, ok, tx, ty, src, dst in halo_sends():
         back_ok, _, _ = neighbour(-dx, -dy)
@@ -312,34 +316,44 @@
             block = jnp.where(lane < 64, a, b)
             fa[c, k, :, rows:wide] = jnp.where(at_y, gy[c, k], block)
             pp[c, k, :, rows:wide] = jnp.where(lane < 64, pltpu.roll(a, 125, 1), pltpu.roll(b, 127, 1))
-            fa[c, k, cols:high, :] = jnp.where(at_x, gx[pl.ds(c * levels + k, 1), :], fa[c, k, cols:high, :])
+            for m in range(wide // 128):
+                here = slice(m * 128, m * 128 + 128)
+                fa[c, k, cols:high, here] = jnp.where(at_x, gx[m, pl.ds(c * levels + k, 1), :], fa[c, k, cols:high, here])
         return both
 
     lax.fori_loop(0, levels, unpack_y, (side(0), side(1)))
 
-    def advanced(src, k):
-        u, v, t, p = (src[c, k] for c in range(4))
-        above = src[2, jnp.minimum(k + 1, levels - 1)]
-        below = src[2, jnp.maximum(k - 1, 0)]
+    blocks, inner_blocks = wide // 128, rows // 128
+
+    def advanced(src, k, b):
+        at = slice(b * 128, b * 128 + 128)
+        u, v, t, p = (src[c, k, :, at] for c in range(4))
+        above = src[2, jnp.minimum(k + 1, levels - 1), :, at]
+        below = src[2, jnp.maximum(k - 1, 0), :, at]
+        after, before = (b + 1) % blocks * 128, (b - 1) % blocks * 128
 
         def dx(f):
             return pltpu.roll(f, high - 1, 0) - pltpu.roll(f, 1, 0)
 
         def dy(f):
-            return pltpu.roll(f, wide - 1, 1) - pltpu.roll(f, 1, 1)
-
-        ux, vy = dx(u), dy(v)
+            c, value = f
+            ahead = jnp.where(lane == 0, src[c, k, :, after:after + 128], value)
+            behind = jnp.where(lane == 127, src[c, k, :, before:before + 128], value)
+            return pltpu.roll(ahead, 127, 1) - pltpu.roll(behind, 1, 1)
+
+        ux, vy = dx(u), dy((1, v))
         hu, hv = u * (CARRY_RATE * 0.5), v * (CARRY_RATE * 0.5)
         s = SOUND_RATE * 0.5
-        yield u - (hu * ux + hv * dy(u)) - s * dx(p)
-        yield v - (hu * dx(v) + hv * vy) - s * dy(p)
-        yield t - (hu * dx(t) + hv * dy(t)) + MIXING_RATE * (above - 2.0 * t + below)
+        yield u - (hu * ux + hv * dy((0, u))) - s * dx(p)
+        yield v - (hu * dx(v) + hv * vy) - s * dy((3, p))
+        yield t - (hu * dx(t) + hv * dy((2, t))) + MIXING_RATE * (above - 2.0 * t + below)
         yield p - s * (ux + vy)
 
     for src, dst in ((fa, fb), (fb, fa)):
         def step(k, _, src=src, dst=dst):
-            for c, value in enumerate(advanced(src, k)):
-                put(dst, c, k, value)
+            for b in range(blocks):
+                for c, value in enumerate(advanced(src, k, b)):
+                    put(dst, c, k, b, value)
             return 0
 
         lax.fori_loop(0, levels, step, 0)
@@ -352,18 +366,16 @@
     k = lax.broadcasted_iota(jnp.int32, (3 * lx.coarse, 3 * cols), 1)
     triples = jnp.where((k >= 3 * j) & (k < 3 * j + 3), 1.0, 0.0).astype(F32)
 
-    def last_step(k, _):
-        inner = [value[0:cols, 0:rows] for value in advanced(fa, k)]
-        for c in range(4):
-            nest_out[c, k] = inner[c]
-        sums = jnp.dot(jnp.concatenate(inner[:3], axis=0), thirds, precision=lax.Precision.HIGHEST,
+    def last_step(k):
+        for b in range(inner_blocks):
+            for c, value in enumerate(advanced(fa, k, b)):
+                nest_out[c, k, :, b * 128:b * 128 + 128] = value[0:cols, :]
+        inner = [nest_out[c, k] for c in range(3)]
+        sums = jnp.dot(jnp.concatenate(inner, axis=0), thirds, precision=lax.Precision.HIGHEST,
                        preferred_element_type=F32)
         mean = jnp.dot(triples, sums, precision=lax.Precision.HIGHEST, preferred_element_type=F32) * (1.0 / 9.0)
         for c in range(3):
-            coarse[c * levels + k] = mean[c * lx.coarse:(c + 1) * lx.coarse, :]
-        return 0
-
-    lax.fori_loop(0, levels, last_step, 0)
+            coarse[k, c] = mean[c * lx.coarse:(c + 1) * lx.coarse, :]
 
     def back_targets():
         for a in range(lx.slots):
@@ -373,24 +385,27 @@
                 tx, ty = jnp.minimum(tx, lx.last(ix)), jnp.minimum(ty, ly.last(iy))
                 yield ok, a, b, tx, ty, ix - lx.base(tx), iy - ly.base(ty)
 
-    for ok, a, b, tx, ty, sx, sy in back_targets():
-        send(ok, coarse, back.at[sx, sy], s_back.at[a, b], r_back.at[sx, sy], tx, ty)
+    pair = 2
+
+    def last_steps(q, _):
+        for m in range(pair):
+            last_step(q * pair + m)
+        now = pl.ds(q * pair, pair)
+        for ok, a, b, tx, ty, sx, sy in back_targets():
+            send(ok, coarse.at[now], back.at[sx, sy, now], s_back.at[a, b, q], r_back.at[sx, sy, q], tx, ty)
+        return 0
+
+    lax.fori_loop(0, levels // pair, last_steps, 0)
 
     def parent_step(k, _):
-        for c, value in enumerate(advanced(pp, k)):
-            parent_out[c, k] = value[0:lx.parent, 0:ly.parent]
+        for b in range(inner_blocks):
+            for c, value in enumerate(advanced(pp, k, b)):
+                parent_out[c, k, :, b * 128:b * 128 + 128] = value[0:lx.parent, :]
         return 0
 
     lax.fori_loop(0, levels, parent_step, 0)
 
     takes_back = in_rows & in_cols
-    for a in range(lx.sources):
-        for b in range(ly.sources):
-            sx, sy = lx.base(ix) + a, ly.base(iy) + b
-            sxc, syc = jnp.clip(sx, 0, lx.count - 1), jnp.clip(sy, 0, ly.count - 1)
-            ok = takes_back & (sx == sxc) & (sy == syc)
-            ok = ok & (ix >= lx.first(sxc)) & (ix <= lx.last(sxc)) & (iy >= ly.first(syc)) & (iy <= ly.last(syc))
-            arrived(ok, back.at[a, b], r_back.at[a, b], blank=False)
 
     @pl.when(takes_back)
     def _():
@@ -399,20 +414,30 @@
         inside = (col >= 0) & (col < lx.span) & (row >= 0) & (row < ly.span)
         x0 = lx.parent * ix - lx.coarse * lx.base(ix) - ox
         y0 = ly.parent * iy - ly.coarse * ly.base(iy) - oy
-        total = lx.window
-        nsy = ly.window // ly.coarse
-
-        def body(k, _):
-            for c in range(3):
-                f = c * levels + k
-                whole = jnp.concatenate(
-                    [jnp.concatenate([back[a, b, f] for b in range(nsy)], axis=1) for a in range(total // lx.coarse)],
-                    axis=0)
-                moved = pltpu.roll(pltpu.roll(whole, total - x0, 0), nsy * ly.coarse - y0, 1)
-                parent_out[c, k] = jnp.where(inside, moved[0:lx.parent, 0:ly.parent], parent_out[c, k])
+        nsx, nsy = lx.window // lx.coarse, ly.window // ly.coarse
+
+        def body(q, _):
+            now = pl.ds(q * pair, pair)
+            for a in range(lx.sources):
+                for b in range(ly.sources):
+                    sx, sy = lx.base(ix) + a, ly.base(iy) + b
+                    sxc, syc = jnp.clip(sx, 0, lx.count - 1), jnp.clip(sy, 0, ly.count - 1)
+                    ok = (sx == sxc) & (sy == syc)
+                    ok = ok & (ix >= lx.first(sxc)) & (ix <= lx.last(sxc))
+                    ok = ok & (iy >= ly.first(syc)) & (iy <= ly.last(syc))
+                    arrived(ok, back.at[a, b, now], r_back.at[a, b, q], blank=False)
+            for m in range(pair):
+                k = q * pair + m
+                for c in range(3):
+                    whole = jnp.concatenate(
+                        [jnp.concatenate([back[a, b, k, c] for b in range(nsy)], axis=1) for a in range(nsx)],
+                        axis=0)
+                    moved = pltpu.roll(whole, lx.window - x0, 0)[0:lx.parent, :]
+                    moved = pltpu.roll(moved, ly.window - y0, 1)
+                    parent_out[c, k] = jnp.where(inside, moved[:, 0:ly.parent], parent_out[c, k])
             return 0
 
-        lax.fori_loop(0, levels, body, 0)
+        lax.fori_loop(0, levels // pair, body, 0)
 
     for ok, j, ty, part in col_targets():
         sent(ok, cs, s_col.at[j], col_to, ty)
@@ -420,8 +445,10 @@
         sent(ok, rs, s_row.at[j], tx, row_to)
     for n, dx, dy, ok, tx, ty, src, dst in halo_sends():
         sent(ok, src, s_halo.at[n], tx, ty)
-    for ok, a, b, tx, ty, sx, sy in back_targets():
-        sent(ok, coarse, s_back.at[a, b], tx, ty)
+    for q in range(levels // pair):
+        now = pl.ds(q * pair, pair)
+        for ok, a, b, tx, ty, sx, sy in back_targets():
+            sent(ok, coarse.at[now], s_back.at[a, b, q], tx, ty)
 
 
 def on_device(lx, ly, nest_state, parent_state, offset_x, offset_y):
@@ -450,14 +477,14 @@
             pltpu.VMEM((n_col, ly.slots, 4 * levels, ly.parent), F32),
             pltpu.VMEM((lx.parent, 128), F32),
             pltpu.VMEM((lx.slots, lx.parent, 128), F32),
-            pltpu.VMEM((4 * levels, wide), F32),
+            pltpu.VMEM((wide // 128, 4 * levels, 128), F32),
             pltpu.VMEM((4, levels, high, 128), F32),
-            pltpu.VMEM((3 * levels, lx.coarse, ly.coarse), F32),
-            pltpu.VMEM((nbx, nby, 3 * levels, lx.coarse, ly.coarse), F32),
+            pltpu.VMEM((levels, 3, lx.coarse, ly.coarse), F32),
+            pltpu.VMEM((nbx, nby, levels, 3, lx.coarse, ly.coarse), F32),
             dma((8,)), dma((8,)),
             dma((ly.sources,)), dma((n_col, ly.slots)),
             dma((lx.sources,)), dma((lx.slots,)),
-            dma((lx.slots, ly.slots)), dma((nbx, nby)),
+            dma((lx.slots, ly.slots, levels // 2)), dma((nbx, nby, levels // 2)),
         ],
         compiler_params=pltpu.CompilerParams(has_side_effects=True, vmem_limit_bytes=48 * 1024 * 1024),
     )(offset_x, offset_y, nest_state, parent_state)

time: 45.6 us -> 41.3 us (0.906)
  Pallas kernels: 38.9 us -> 34.6 us
    pallas_call x1, Pallas kernels: 38.9 us -> 34.6 us  [on_device(): pl.pallas_call(functools.partial(kernel, lx, ly, levels), out_shape=(shap...]
where the time goes in v2:
time: 41.3 us; the launch traced here: 41.1 us
  Pallas kernels  34.6 us (84%)
  local copies, waits for them, and re-layouts  4.56 us (11%)
  between operations  1.94 us (5%)
    pallas_call x1, Pallas kernels, on_device(): pl.pallas_call(functools.partial(kernel, lx, ly, levels), out_shape=(shap...  34.6 us
    unnamed x6, local copies, waits for them, and re-layouts  4.56 us

profile of v2, /device:TPU:9, one launch (start us, length us, event | category | flops | bytes accessed | tf_op | source)
XLA Modules:
  0.0 41.1 jit_solution(6478363855992995567)
XLA Ops:
  1.9 0.0 copy-start
  1.9 1.3 %copy-done = f32[4,8,24,384]{3,2,1,0:T(8,128)S(1)} copy-done((f32[4,8,24,384]{3,2,1,0:T(8,128)S(1)}, f32[4,8,24,384]{3,2,1,0:T(8,128)}, u32[]{:S(2)}) %copy-start) | copy-done | bytes 1179672
  3.2 0.0 copy-start.1
  3.2 1.3 %copy-done.1 = f32[4,8,24,384]{3,2,1,0:T(8,128)S(1)} copy-done((f32[4,8,24,384]{3,2,1,0:T(8,128)S(1)}, f32[4,8,24,384]{3,2,1,0:T(8,128)}, u32[]{:S(2)}) %copy-start.1) | copy-done | bytes 1179672
  4.5 34.6 %shard_map.59 = (f32[4,8,24,384]{3,2,1,0:T(8,128)S(1)}, f32[4,8,24,384]{3,2,1,0:T(8,128)S(1)}) custom-call(s32[1]{0:T(128)S(6)} %copy.8.off_x, s32[1]{0:T(128)S(6)} %copy.9.off_y, f32[4,8,24,384]{3,2,1,0:T(8,128)S(1)} %copy-done, f32[4,8,24,384]{3,2,1,0:T(8,128)S(1)} %copy-done.1), custom_call_target="tpu_custom_call" | custom-call | tf_op jit(solution)/shard_map/pallas_call | solution.py:465
  39.1 1.0 %copy.10 = f32[4,8,24,384]{3,2,1,0:T(8,128)} copy(f32[4,8,24,384]{3,2,1,0:T(8,128)S(1)} %get-tuple-element.4) | data formatting | bytes 2359296
  40.1 1.0 %copy.11 = f32[4,8,24,384]{3,2,1,0:T(8,128)} copy(f32[4,8,24,384]{3,2,1,0:T(8,128)S(1)} %get-tuple-element.5) | data formatting | bytes 2359296
Async XLA Ops:
  1.9 1.3 %copy-start = (f32[4,8,24,384]{3,2,1,0:T(8,128)S(1)}, f32[4,8,24,384]{3,2,1,0:T(8,128)}, u32[]{:S(2)}) copy-start(f32[4,8,24,384]{3,2,1,0:T(8,128)} %nest.1) | copy-start | bytes 3538948
  3.2 1.3 %copy-start.1 = (f32[4,8,24,384]{3,2,1,0:T(8,128)S(1)}, f32[4,8,24,384]{3,2,1,0:T(8,128)}, u32[]{:S(2)}) copy-start(f32[4,8,24,384]{3,2,1,0:T(8,128)} %parent.1) | copy-start | bytes 3538948

commit v3 on v2

--- a/solution.py
+++ b/solution.py
@@ -107,20 +107,6 @@
     gives_row = in_cols & (gives_south | gives_north)
     row_to = jnp.where(gives_south, 0, ly.count - 1)
 
-    @pl.when(gives_col)
-    def _():
-        want = ox + jnp.where(gives_west, -1, lx.span) - lx.parent * ix
-        sub = lax.broadcasted_iota(jnp.int32, (lx.parent, ly.parent), 0)
-        hit = sub == want
-
-        def body(k, _):
-            for c in range(4):
-                line = jnp.sum(jnp.where(hit, parent[c, k], 0.0), axis=0, keepdims=True)
-                cs[pl.ds(c * levels + k, 1), :] = line
-            return 0
-
-        lax.fori_loop(0, levels, body, 0)
-
     def col_targets():
         for j in range(ly.sources):
             ty = ly.base(iy) + j
@@ -128,47 +114,12 @@
             ok = gives_col & (ty >= 0) & (ty < ly.count) & (iy >= ly.first(tyc)) & (iy <= ly.last(tyc))
             yield ok, j, tyc, jnp.clip(iy - ly.first(tyc), 0, ly.slots - 1)
 
-    for ok, j, ty, part in col_targets():
-        slot = jnp.clip(col_slot, 0, n_col - 1)
-        send(ok, cs, cr.at[slot, part], s_col.at[j], r_col.at[slot, part], col_to, ty)
-
-    @pl.when(gives_row)
-    def _():
-        want = oy + jnp.where(gives_south, -1, ly.span) - ly.parent * iy
-        hit = lax.broadcasted_iota(jnp.int32, (lx.parent, ly.parent), 1) == want
-
-        def body(k, acc):
-            for c in range(4):
-                line = jnp.sum(jnp.where(hit, parent[c, k], 0.0), axis=1, keepdims=True)
-                acc = jnp.where(lane == c * levels + k, line, acc)
-            return acc
-
-        rs[...] = lax.fori_loop(0, levels, body, jnp.zeros((lx.parent, 128), F32))
-
     def row_targets():
         for j in range(lx.sources):
             tx = lx.base(ix) + j
             txc = jnp.clip(tx, 0, lx.count - 1)
             ok = gives_row & (tx >= 0) & (tx < lx.count) & (ix >= lx.first(txc)) & (ix <= lx.last(txc))
             yield ok, j, txc, jnp.clip(ix - lx.first(txc), 0, lx.slots - 1)
-
-    for ok, j, tx, part in row_targets():
-        send(ok, rs, rr.at[part], s_row.at[j], r_row.at[part], tx, row_to)
-
-    half = levels // 2
-
-    def pack_x(k, _):
-        for c in range(4):
-            for part in range(2):
-                lev = k + part * half
-                r = 4 * part
-                xs[0, c, k, r:r + 3, :] = nest[c, lev, 0:3, :]
-                xs[0, c, k, r + 3:r + 4, :] = parent[c, lev, 0:1, :]
-                xs[1, c, k, r:r + 3, :] = nest[c, lev, cols - 3:cols, :]
-                xs[1, c, k, r + 3:r + 4, :] = parent[c, lev, cols - 1:cols, :]
-        return 0
-
-    lax.fori_loop(0, half, pack_x, 0)
 
     has = {-1: lambda i, n: i > 0, 0: lambda i, n: i >= 0, 1: lambda i, n: i < n - 1}
 
@@ -191,9 +142,85 @@
                     src, dst = ys.at[d, pl.ds(cols - 8, 8)], yr.at[d, pl.ds(cols + 8, 8)]
             yield n, dx, dy, ok, tx, ty, src, dst
 
+    def back_targets():
+        for a in range(lx.slots):
+            for b in range(ly.slots):
+                tx, ty = lx.first(ix) + a, ly.first(iy) + b
+                ok = (tx <= lx.last(ix)) & (ty <= ly.last(iy))
+                tx, ty = jnp.minimum(tx, lx.last(ix)), jnp.minimum(ty, ly.last(iy))
+                yield ok, a, b, tx, ty, ix - lx.base(tx), iy - ly.base(ty)
+
+    takes_back = in_rows & in_cols
+    west, east = ix == 0, ix == lx.count - 1
+    south, north = iy == 0, iy == ly.count - 1
+    takes_col = west | east
+    takes_row = south | north
+
+    def col_slots():
+        for s in range(n_col):
+            live = (west & (s < n_before)) | (east & (s < n_after))
+            tx = jnp.where(west, lx.before[0] + s, lx.after[0] + s)
+            for part in range(ly.slots):
+                ok = live & (ly.first(iy) + part <= ly.last(iy))
+                yield ok, s, part, jnp.minimum(tx, lx.count - 1), jnp.minimum(ly.first(iy) + part, ly.last(iy))
+
+    def row_slots():
+        for part in range(lx.slots):
+            ok = takes_row & (lx.first(ix) + part <= lx.last(ix))
+            yield ok, part, jnp.minimum(lx.first(ix) + part, lx.last(ix)), jnp.where(south, ly.before[0], ly.after[0])
+
+    def back_slots():
+        for a in range(lx.sources):
+            for b in range(ly.sources):
+                sx, sy = lx.base(ix) + a, ly.base(iy) + b
+                sxc, syc = jnp.clip(sx, 0, lx.count - 1), jnp.clip(sy, 0, ly.count - 1)
+                ok = takes_back & (sx == sxc) & (sy == syc)
+                ok = ok & (ix >= lx.first(sxc)) & (ix <= lx.last(sxc))
+                ok = ok & (iy >= ly.first(syc)) & (iy <= ly.last(syc))
+                yield ok, a, b, sxc, syc
+
+    barrier = pltpu.get_barrier_semaphore()
+
+    def greet(ok, tx, ty):
+        @pl.when(ok & jnp.logical_not((tx == ix) & (ty == iy)))
+        def _():
+            pl.semaphore_signal(barrier, inc=1, device_id=there(tx, ty), device_id_type=MESH)
+
+    expected = jnp.int32(0)
+
+    def count(ok, tx, ty):
+        return jnp.where(ok & jnp.logical_not((tx == ix) & (ty == iy)), 1, 0).astype(jnp.int32)
+
     for n, dx, dy, ok, tx, ty, src, dst in halo_sends():
-        if dy == 0:
-            send(ok, src, dst, s_halo.at[n], r_halo.at[n], tx, ty, local=False)
+        greet(ok, tx, ty)
+        expected = expected + count(ok, tx, ty)
+    for ok, s, part, tx, ty in col_slots():
+        greet(ok, tx, ty)
+    for ok, part, tx, ty in row_slots():
+        greet(ok, tx, ty)
+    for ok, a, b, tx, ty in back_slots():
+        greet(ok, tx, ty)
+    for ok, j, ty, part in col_targets():
+        expected = expected + count(ok, col_to, ty)
+    for ok, j, tx, part in row_targets():
+        expected = expected + count(ok, tx, row_to)
+    for ok, a, b, tx, ty, sx, sy in back_targets():
+        expected = expected + count(ok, tx, ty)
+
+    half = levels // 2
+
+    def pack_x(k, _):
+        for c in range(4):
+            for part in range(2):
+                lev = k + part * half
+                r = 4 * part
+                xs[0, c, k, r:r + 3, :] = nest[c, lev, 0:3, :]
+                xs[0, c, k, r + 3:r + 4, :] = parent[c, lev, 0:1, :]
+                xs[1, c, k, r:r + 3, :] = nest[c, lev, cols - 3:cols, :]
+                xs[1, c, k, r + 3:r + 4, :] = parent[c, lev, cols - 1:cols, :]
+        return 0
+
+    lax.fori_loop(0, half, pack_x, 0)
 
     def pack_y(k, acc):
         low, top = acc
@@ -211,9 +238,43 @@
     low, top = lax.fori_loop(0, levels, pack_y, (blank, blank))
     ys[0] = low
     ys[1] = top
+    pl.semaphore_wait(barrier, expected)
     for n, dx, dy, ok, tx, ty, src, dst in halo_sends():
-        if dy != 0:
-            send(ok, src, dst, s_halo.at[n], r_halo.at[n], tx, ty, local=False)
+        send(ok, src, dst, s_halo.at[n], r_halo.at[n], tx, ty, local=False)
+
+    @pl.when(gives_col)
+    def _():
+        want = ox + jnp.where(gives_west, -1, lx.span) - lx.parent * ix
+        sub = lax.broadcasted_iota(jnp.int32, (lx.parent, ly.parent), 0)
+        hit = sub == want
+
+        def body(k, _):
+            for c in range(4):
+                line = jnp.sum(jnp.where(hit, parent[c, k], 0.0), axis=0, keepdims=True)
+                cs[pl.ds(c * levels + k, 1), :] = line
+            return 0
+
+        lax.fori_loop(0, levels, body, 0)
+
+    for ok, j, ty, part in col_targets():
+        slot = jnp.clip(col_slot, 0, n_col - 1)
+        send(ok, cs, cr.at[slot, part], s_col.at[j], r_col.at[slot, part], col_to, ty)
+
+    @pl.when(gives_row)
+    def _():
+        want = oy + jnp.where(gives_south, -1, ly.span) - ly.parent * iy
+        hit = lax.broadcasted_iota(jnp.int32, (lx.parent, ly.parent), 1) == want
+
+        def body(k, acc):
+            for c in range(4):
+                line = jnp.sum(jnp.where(hit, parent[c, k], 0.0), axis=1, keepdims=True)
+                acc = jnp.where(lane == c * levels + k, line, acc)
+            return acc
+
+        rs[...] = lax.fori_loop(0, levels, body, jnp.zeros((lx.parent, 128), F32))
+
+    for ok, j, tx, part in row_targets():
+        send(ok, rs, rr.at[part], s_row.at[j], r_row.at[part], tx, row_to)
 
     def middle(k, _):
         for c in range(4):
@@ -223,16 +284,10 @@
 
     lax.fori_loop(0, levels, middle, 0)
 
-    west, east = ix == 0, ix == lx.count - 1
-    south, north = iy == 0, iy == ly.count - 1
-    takes_col = west | east
-    takes_row = south | north
-    for s in range(n_col):
-        live = (west & (s < n_before)) | (east & (s < n_after))
-        for part in range(ly.slots):
-            arrived(live & (ly.first(iy) + part <= ly.last(iy)), cr.at[s, part], r_col.at[s, part])
-    for part in range(lx.slots):
-        arrived(takes_row & (lx.first(ix) + part <= lx.last(ix)), rr.at[part], r_row.at[part])
+    for ok, s, part, tx, ty in col_slots():
+        arrived(ok, cr.at[s, part], r_col.at[s, part])
+    for ok, part, tx, ty in row_slots():
+        arrived(ok, rr.at[part], r_row.at[part])
 
     def third(v):
         return (((v + 3) * 21846) >> 16) - 1
@@ -377,14 +432,6 @@
         for c in range(3):
             coarse[k, c] = mean[c * lx.coarse:(c + 1) * lx.coarse, :]
 
-    def back_targets():
-        for a in range(lx.slots):
-            for b in range(ly.slots):
-                tx, ty = lx.first(ix) + a, ly.first(iy) + b
-                ok = (tx <= lx.last(ix)) & (ty <= ly.last(iy))
-                tx, ty = jnp.minimum(tx, lx.last(ix)), jnp.minimum(ty, ly.last(iy))
-                yield ok, a, b, tx, ty, ix - lx.base(tx), iy - ly.base(ty)
-
     pair = 2
 
     def last_steps(q, _):
@@ -404,8 +451,6 @@
         return 0
 
     lax.fori_loop(0, levels, parent_step, 0)
-
-    takes_back = in_rows & in_cols
 
     @pl.when(takes_back)
     def _():
@@ -418,14 +463,8 @@
 
         def body(q, _):
             now = pl.ds(q * pair, pair)
-            for a in range(lx.sources):
-                for b in range(ly.sources):
-                    sx, sy = lx.base(ix) + a, ly.base(iy) + b
-                    sxc, syc = jnp.clip(sx, 0, lx.count - 1), jnp.clip(sy, 0, ly.count - 1)
-                    ok = (sx == sxc) & (sy == syc)
-                    ok = ok & (ix >= lx.first(sxc)) & (ix <= lx.last(sxc))
-                    ok = ok & (iy >= ly.first(syc)) & (iy <= ly.last(syc))
-                    arrived(ok, back.at[a, b, now], r_back.at[a, b, q], blank=False)
+            for ok, a, b, sx, sy in back_slots():
+                arrived(ok, back.at[a, b, now], r_back.at[a, b, q], blank=False)
             for m in range(pair):
                 k = q * pair + m
                 for c in range(3):
@@ -486,7 +525,7 @@
             dma((lx.sources,)), dma((lx.slots,)),
             dma((lx.slots, ly.slots, levels // 2)), dma((nbx, nby, levels // 2)),
         ],
-        compiler_params=pltpu.CompilerParams(has_side_effects=True, vmem_limit_bytes=48 * 1024 * 1024),
+        compiler_params=pltpu.CompilerParams(collective_id=0, has_side_effects=True, vmem_limit_bytes=48 * 1024 * 1024),
     )(offset_x, offset_y, nest_state, parent_state)
 
 

time: 41.3 us -> 37.9 us (0.918)
  Pallas kernels: 34.6 us -> 31.2 us
    pallas_call x1, Pallas kernels: 34.6 us -> 31.2 us  [on_device(): pl.pallas_call(functools.partial(kernel, lx, ly, levels), out_shape=(shap...]
where the time goes in v3:
time: 37.9 us; the launch traced here: 37.7 us
  Pallas kernels  31.2 us (82%)
  local copies, waits for them, and re-layouts  4.56 us (12%)
  between operations  1.94 us (5%)
    pallas_call x1, Pallas kernels, on_device(): pl.pallas_call(functools.partial(kernel, lx, ly, levels), out_shape=(shap...  31.2 us
    unnamed x6, local copies, waits for them, and re-layouts  4.56 us

profile of v3, /device:TPU:9, one launch (start us, length us, event | category | flops | bytes accessed | tf_op | source)
XLA Modules:
  0.0 37.7 jit_solution(9159209989947091784)
XLA Ops:
  1.9 0.0 copy-start
  1.9 1.3 %copy-done = f32[4,8,24,384]{3,2,1,0:T(8,128)S(1)} copy-done((f32[4,8,24,384]{3,2,1,0:T(8,128)S(1)}, f32[4,8,24,384]{3,2,1,0:T(8,128)}, u32[]{:S(2)}) %copy-start) | copy-done | bytes 1179672
  3.2 0.0 copy-start.1
  3.2 1.3 %copy-done.1 = f32[4,8,24,384]{3,2,1,0:T(8,128)S(1)} copy-done((f32[4,8,24,384]{3,2,1,0:T(8,128)S(1)}, f32[4,8,24,384]{3,2,1,0:T(8,128)}, u32[]{:S(2)}) %copy-start.1) | copy-done | bytes 1179672
  4.5 31.2 %shard_map.59 = (f32[4,8,24,384]{3,2,1,0:T(8,128)S(1)}, f32[4,8,24,384]{3,2,1,0:T(8,128)S(1)}) custom-call(s32[1]{0:T(128)S(6)} %copy.8.off_x, s32[1]{0:T(128)S(6)} %copy.9.off_y, f32[4,8,24,384]{3,2,1,0:T(8,128)S(1)} %copy-done, f32[4,8,24,384]{3,2,1,0:T(8,128)S(1)} %copy-done.1), custom_call_target="tpu_custom_call" | custom-call | tf_op jit(solution)/shard_map/pallas_call | solution.py:504
  35.6 1.0 %copy.10 = f32[4,8,24,384]{3,2,1,0:T(8,128)} copy(f32[4,8,24,384]{3,2,1,0:T(8,128)S(1)} %get-tuple-element.4) | data formatting | bytes 2359296
  36.7 1.0 %copy.11 = f32[4,8,24,384]{3,2,1,0:T(8,128)} copy(f32[4,8,24,384]{3,2,1,0:T(8,128)S(1)} %get-tuple-element.5) | data formatting | bytes 2359296
Async XLA Ops:
  1.9 1.3 %copy-start = (f32[4,8,24,384]{3,2,1,0:T(8,128)S(1)}, f32[4,8,24,384]{3,2,1,0:T(8,128)}, u32[]{:S(2)}) copy-start(f32[4,8,24,384]{3,2,1,0:T(8,128)} %nest.1) | copy-start | bytes 3538948
  3.2 1.3 %copy-start.1 = (f32[4,8,24,384]{3,2,1,0:T(8,128)S(1)}, f32[4,8,24,384]{3,2,1,0:T(8,128)}, u32[]{:S(2)}) copy-start(f32[4,8,24,384]{3,2,1,0:T(8,128)} %parent.1) | copy-start | bytes 3538948
